TPU v7x, 256 devices: a whole 4x4x8 slice. The times are simulated.
256 devices in a mesh: dom: 64 (over y, z, core), grp: 4 (over x).
Axes of the slice: x: 4, y: 4, z: 8, core: 2. Of those that a mesh axis runs over, the one named last changes fastest.
Arguments:
- a_tiles: bfloat16 [64, 4, 18, 8, 128, 128], P('dom', 'grp'), as said below
- columns: int32 [64, 4, 18, 8], P('dom', 'grp'), may hold values from 0 to 59, as said below
- surplus_tiles: bfloat16 [64, 4, 6, 8, 128, 128], P('dom', 'grp'), as said below
- surplus_cols: int32 [64, 4, 6, 8], P('dom', 'grp'), may hold values from 0 to 59, as said below
- hosts: int32 [64, 4], P('dom', 'grp'), may hold values from -1 to 2, as said below
- counts: int32 [64, 4], P('dom', 'grp'), may hold values from 6 to 36, as said below
- send_ids: int32 [64, 4, 4, 6], P('dom', 'grp'), may hold values from -1 to 35, as said below
- p0: bfloat16 [64, 4, 36, 96, 128], P('dom', 'grp'), may hold values from -6 to 6
Outputs:
- p_smooth: bfloat16 [64, 4, 36, 96, 128], P('dom', 'grp')
Inputs may be any that keep to these rules, and one draw needn't show every extreme that they name: `counts`: in each group of 4 partitions with one dom index, exactly one partition holds 36 tile rows; the others hold 6 to 12. `hosts`: in each group, the partition that holds 36 tile rows has -1; the other three have 0, 1 and 2, each once. send_ids[p, g, j] lists distinct live tile rows of partition (p, g) that partition (p + o_j, g) needs, o = (1, -1, 4, -4); used entries come first and -1 fills the rest; lists toward a partition outside the grid, or for o = 1 or -1 outside the same run of 4 dom indices, are all -1; some list is full in every draw. `columns`: for a live row r below 18 of partition (p, g), slot 0 names r itself; every other slot names a live tile row of the partition or the entry 36 + j * 6 + s for a used entry s of send_ids[p - o_j, g, j]. Other rows name 0 in every slot. `surplus_cols`: for a partition (p, g) with hosts[p, g] = b >= 0, row s describes tile row 18 + b * 6 + s of the group's heaviest partition: slot 0 names that row, every other slot a live tile row of that partition or an entry of its extended list as for columns. The heaviest partition's rows name 0. For a live row r below 18, the diagonal entries of a_tiles[p, g, r, 0] lie between 1 and 2; all tiles of other rows are zero. For a partition with hosts[p, g] >= 0, the diagonal entries of surplus_tiles[p, g, s, 0] lie between 1 and 2; the heaviest partition's surplus_tiles are zero.
All inputs are finite; a program needn't handle non-finite values.
Results may differ from a plain program's by a relative error of at most 0.001.
Values may be sent and summed in bfloat16 or wider, within the bound.
A program may use at most 192 MiB of HBM per device.

v0:
```python
import jax
import jax.numpy as jnp
from jax import lax
from jax.sharding import PartitionSpec as P

PW = 4


def from_behind(value, axis, steps):
    count = lax.axis_size(axis)
    initial, last = (max(0, -steps), min(count, count - steps))
    return lax.ppermute(value, axis, [(source, source + steps) for source in range(initial, last)])


def spread(x, axis, root):
    mine = lax.axis_index(axis) == root
    return lax.psum(jnp.where(mine, x, jnp.zeros_like(x)), axis)


def tile_products(matrix_tiles, gathered):
    return jnp.einsum("rkcm,rkim->rci", gathered, matrix_tiles, preferred_element_type=jnp.float32)


def row_bound(tiles, live_rows):
    diagonal = jnp.diagonal(tiles[:, 0], axis1=1, axis2=2).astype(jnp.float32)
    abs_sums = jnp.sum(jnp.abs(tiles), axis=(1, 3), dtype=jnp.float32)
    safe_diag = jnp.where(live_rows[:, None], diagonal, 1.0)
    return (jnp.max(jnp.where(live_rows[:, None], abs_sums / safe_diag, 0.0)), diagonal)


def block_holders(blocks, block_count):
    members = jnp.arange(blocks.shape[0], dtype=jnp.int32)
    return jnp.stack(
        [jnp.sum(jnp.where(blocks == index_b, members, 0)) for index_b in range(block_count)]
    )


def on_device(a_tiles, columns, surplus_tiles, surplus_cols, hosts, counts, send_ids, p0):
    matrix_tiles = a_tiles[0, 0]
    slot_cols = columns[0, 0]
    guest_tiles = surplus_tiles[0, 0]
    guest_cols = surplus_cols[0, 0]
    my_block = hosts[0, 0]
    my_rows = counts[0, 0]
    send_lists = send_ids[0, 0]
    own_p0 = p0[0, 0]
    stored = matrix_tiles.shape[0]
    block_rows = guest_tiles.shape[0]
    capacity = own_p0.shape[0]
    tail_rows = capacity - stored
    tail_blocks = tail_rows // block_rows
    stored_live = jnp.arange(stored) < my_rows
    guest_live = jnp.broadcast_to(my_block >= 0, (block_rows,))
    stored_bound, stored_diag = row_bound(matrix_tiles, stored_live)
    guest_bound, guest_diag = row_bound(guest_tiles, guest_live)
    local_bound = jnp.maximum(stored_bound, guest_bound)
    global_bound = lax.pmax(local_bound, ("dom", "grp"))
    damping = 4.0 / (3.0 * global_bound)
    pieces = [own_p0]
    for direction, offset in enumerate((1, -1, PW, -PW)):
        row_names = send_lists[direction]
        neighbour = from_behind(own_p0, "dom", offset)
        their_names = from_behind(row_names, "dom", offset)
        chosen = neighbour[jnp.clip(their_names, 0, capacity - 1)]
        pieces.append(jnp.where((their_names >= 0)[:, None, None], chosen, jnp.zeros_like(chosen)))
    extended = jnp.concatenate(pieces, axis=0)
    own_products = tile_products(matrix_tiles, extended[slot_cols])
    blocks = lax.all_gather(jnp.reshape(my_block, (1,)), "grp", axis=0, tiled=True)
    members = jnp.arange(blocks.shape[0], dtype=jnp.int32)
    heavy_index = jnp.sum(jnp.where(blocks < 0, members, 0))
    shared = spread(extended, "grp", heavy_index)
    guest_products = tile_products(guest_tiles, shared[guest_cols])
    back_products, back_diag = (
        lax.all_gather(guest_products[None], "grp", axis=0, tiled=True),
        lax.all_gather(guest_diag[None], "grp", axis=0, tiled=True),
    )
    holder = block_holders(blocks, tail_blocks)
    tail_products = back_products[holder].reshape((tail_rows,) + guest_products.shape[1:])
    tail_diag = back_diag[holder].reshape(tail_rows, guest_diag.shape[1])
    products = jnp.concatenate([own_products, tail_products], axis=0)
    diagonal = jnp.concatenate([stored_diag, tail_diag], axis=0)
    live_rows = jnp.arange(capacity) < my_rows
    safe_diag = jnp.where(live_rows[:, None], diagonal, 1.0)
    inv_diag = 1.0 / safe_diag
    result = own_p0.astype(jnp.float32) - damping * inv_diag[:, None, :] * products
    smoothed = jnp.where(live_rows[:, None, None], result, 0.0).astype(jnp.bfloat16)
    return smoothed[None, None]


def solution(mesh):
    in_specs = (
        P("dom", "grp", None, None, None, None),
        P("dom", "grp", None, None),
        P("dom", "grp", None, None, None, None),
        P("dom", "grp", None, None),
        P("dom", "grp"),
        P("dom", "grp"),
        P("dom", "grp", None, None),
        P("dom", "grp", None, None, None),
    )
    out_specs = P("dom", "grp", None, None, None)
    return jax.shard_map(
        on_device, mesh=mesh, in_specs=in_specs, out_specs=out_specs, check_vma=False
    )
```

profile of v0, /device:TPU:32, one launch (start us, length us, event | category | flops | bytes accessed | tf_op | source)
XLA Modules:
  0.0 277.1 jit_solution(542297062606704210)
XLA Ops:
  6.5 2.0 collective-permute-start.1
  8.6 3.6 %collective-permute-start.3 = (bf16[36,96,128]{2,1,0:T(8,128)(2,1)}, bf16[36,96,128]{2,1,0:T(8,128)(2,1)}, u32[]{:S(2)}, u32[]{:S(2)}) collective-permute-start(bf16[36,96,128]{2,1,0:T(8,128)(2,1)} %bitcast.84), channel_id=1, source_target_pairs={{4,0},{8,4},{12,8},{16,12},{20,16},{24,20},{28,24},{32,28},{36,32}... | collective-permute-start | bytes 2654216 | tf_op jit(solution)/shard_map/ppermute | solution.py:12
  12.2 6.1 %collective-permute-start.5 = (bf16[36,96,128]{2,1,0:T(8,128)(2,1)}, bf16[36,96,128]{2,1,0:T(8,128)(2,1)}, u32[]{:S(2)}, u32[]{:S(2)}) collective-permute-start(bf16[36,96,128]{2,1,0:T(8,128)(2,1)} %bitcast.85), channel_id=1, source_target_pairs={{0,16},{4,20},{8,24},{12,28},{16,32},{20,36},{24,40},{28,44},{32,4... | collective-permute-start | bytes 2654216 | tf_op jit(solution)/shard_map/ppermute | solution.py:12
  20.5 3.1 %collective-permute-start = (s32[6]{0:T(128)S(1)}, s32[6]{0:T(128)S(1)}, u32[]{:S(2)}, u32[]{:S(2)}) collective-permute-start(s32[6]{0:T(128)S(1)} %get-tuple-element.11), channel_id=1, source_target_pairs={{0,4},{4,8},{8,12},{12,16},{16,20},{20,24},{24,28},{28,32},{32,36}... | collective-permute-start | bytes 80 | tf_op jit(solution)/shard_map/ppermute | solution.py:12
  27.5 8.9 %all-reduce = s32[4]{0:T(128)S(1)} all-reduce(s32[4]{0:T(128)S(1)} %bitcast_dynamic-update-slice_fusion), channel_id=3, replica_groups=mesh['dom'=64,'grp'=4] {'grp'}, use_global_device_ids=true, to_apply=%add | all-reduce | flops 4 | bytes 32
  37.1 23.1 %copy.24 = bf16[1,1,6,8,128,128]{2,5,4,3,1,0:T(8,128)(2,1)} copy(bf16[1,1,6,8,128,128]{5,4,3,2,1,0:T(8,128)(2,1)S(1)} %copy-done) | data formatting | bytes 3145728 | tf_op args[2]
  60.2 12.0 %convert_reduce_fusion = f32[6,128]{0,1:T(8,128)} fusion(bf16[1,1,6,8,128,128]{2,5,4,3,1,0:T(8,128)(2,1)} %copy.24), kind=kLoop, calls=%fused_computation.10 | loop fusion | flops 2358528 | bytes 1575936 | tf_op jit(solution)/shard_map/reduce_sum | solution.py:26
  72.3 27.9 %copy.23 = bf16[1,1,18,8,128,128]{2,5,4,3,1,0:T(8,128)(2,1)} copy(bf16[1,1,18,8,128,128]{5,4,3,2,1,0:T(8,128)(2,1)} %param.8) | data formatting | bytes 9437184 | tf_op args[0]
  100.2 12.1 %convert_reduce_fusion.1 = f32[18,128]{0,1:T(8,128)} fusion(bf16[1,1,18,8,128,128]{2,5,4,3,1,0:T(8,128)(2,1)} %copy.23), kind=kLoop, calls=%fused_computation.11 | loop fusion | flops 7075584 | bytes 4727808 | tf_op jit(solution)/shard_map/reduce_sum | solution.py:26
  112.9 1.9 collective-permute-start.2
  116.8 6.4 %collective-permute-start.4 = (s32[6]{0:T(128)S(1)}, s32[6]{0:T(128)S(1)}, u32[]{:S(2)}, u32[]{:S(2)}) collective-permute-start(s32[6]{0:T(128)S(1)} %get-tuple-element.12), channel_id=1, source_target_pairs={{0,16},{4,20},{8,24},{12,28},{16,32},{20,36},{24,40},{28,44},{32,4... | collective-permute-start | bytes 80 | tf_op jit(solution)/shard_map/ppermute | solution.py:12
  125.8 5.2 %collective-permute-done.6 = s32[6]{0:T(128)S(1)} collective-permute-done((s32[6]{0:T(128)S(1)}, s32[6]{0:T(128)S(1)}, u32[]{:S(2)}, u32[]{:S(2)}) %collective-permute-start.6) | collective-permute-done | bytes 56 | tf_op jit(solution)/shard_map/ppermute | solution.py:12
  139.9 4.7 %slice_bitcast_fusion = bf16[6,128,128]{0,2,1:T(8,128)(2,1)} fusion(bf16[6,8,128,128]{0,3,2,1:T(8,128)(2,1)} %bitcast.80), kind=kLoop, calls=%fused_computation.14 | loop fusion | bytes 393216 | tf_op jit(solution)/shard_map/squeeze | solution.py:25
  144.7 1.9 gather_fusion.1
  146.6 4.9 %slice_bitcast_fusion.1 = bf16[18,128,128]{0,2,1:T(8,128)(2,1)} fusion(bf16[18,8,128,128]{0,3,2,1:T(8,128)(2,1)} %bitcast.79), kind=kLoop, calls=%fused_computation.15 | loop fusion | bytes 1179648 | tf_op jit(solution)/shard_map/squeeze | solution.py:25
  151.5 2.1 gather_fusion
  156.6 80.8 %pmax.7 = f32[]{:T(128)} all-reduce(f32[]{:T(128)S(6)} %max.15), channel_id=1, replica_groups=mesh['dom'=64,'grp'=4] {'dom','grp'}, use_global_device_ids=true, to_apply=%region_4.5 | all-reduce | flops 1 | bytes 8 | tf_op jit(solution)/shard_map/pmax | solution.py:57
  237.6 3.1 %gather_fusion.8 = bf16[48,96,128]{2,1,0:T(8,128)(2,1)} fusion(bf16[60,96,128]{2,1,0:T(8,128)(2,1)} %all-reduce.3.cloned.1.call-done, s32[1024]{0:T(1024)S(1)} %pad_clamp_fusion), kind=kCustom, calls=%fused_computation.8 | custom fusion | bytes 2359488 | tf_op jit(solution)/shard_map/gather | solution.py:72
  240.7 2.6 fusion.10
  243.6 11.9 %all-gather.3 = f32[4,6,128]{2,1,0:T(8,128)S(1)} all-gather(f32[1,6,128]{2,1,0:T(8,128)S(1)} %copy.25), channel_id=2, replica_groups=mesh['dom'=64,'grp'=4] {'grp'}, dimensions={0}, use_global_device_ids=true | all-gather | bytes 15360 | tf_op jit(solution)/shard_map/all_gather | solution.py:75
  255.6 2.0 fusion.24
  259.0 3.0 %gather_fusion.7 = bf16[144,96,128]{2,1,0:T(8,128)(2,1)} fusion(bf16[60,96,128]{2,1,0:T(8,128)(2,1)S(1)} %select_dynamic-update-slice_fusion, s32[1024]{0:T(1024)S(1)} %pad_clamp_fusion.1), kind=kCustom, calls=%fused_computation.7 | custom fusion | bytes 7078464 | tf_op jit(solution)/shard_map/gather | solution.py:67
  262.0 5.0 %fusion.7 = f32[1,1,18,96,128]{4,3,2,1,0:T(8,128)S(1)} fusion(bf16[18,8,96,128]{3,2,1,0:T(8,128)(2,1)} %bitcast.81, bf16[1,1,18,8,128,128]{5,4,3,2,1,0:T(8,128)(2,1)} %param.8), kind=kOutput, calls=%fused_computation.23 | convolution fusion | flops 452984832 | bytes 9142272 | tf_op jit(solution)/shard_map/rkcm,rkim->rci/dot_general | solution.py:21
  267.1 1.9 gather_fusion.9
  (75 shorter events, 22.8 us)
Async XLA Ops:
  6.5 30.6 %copy-start = (bf16[1,1,6,8,128,128]{5,4,3,2,1,0:T(8,128)(2,1)S(1)}, bf16[1,1,6,8,128,128]{5,4,3,2,1,0:T(8,128)(2,1)}, u32[]{:S(2)}) copy-start(bf16[1,1,6,8,128,128]{5,4,3,2,1,0:T(8,128)(2,1)} %param.10) | copy-start | bytes 4718596
  6.5 231.1 %all-reduce.3.cloned.1.call-start = ((), (), s32[]{:S(2)}) async-start(), calls=%async_computation | async-start | bytes 2949120 | tf_op jit(solution)/shard_map/psum | solution.py:17
  6.5 124.5 %collective-permute-start.1 = (bf16[36,96,128]{2,1,0:T(8,128)(2,1)}, bf16[36,96,128]{2,1,0:T(8,128)(2,1)}, u32[]{:S(2)}, u32[]{:S(2)}) collective-permute-start(bf16[36,96,128]{2,1,0:T(8,128)(2,1)} %bitcast.83), channel_id=1, source_target_pairs={{0,4},{4,8},{8,12},{12,16},{16,20},{20,24},{24,28},{28,32},{32,36}... | collective-permute-start | bytes 2654216 | tf_op jit(solution)/shard_map/ppermute | solution.py:12
  8.6 124.3 %collective-permute-start.3 = (bf16[36,96,128]{2,1,0:T(8,128)(2,1)}, bf16[36,96,128]{2,1,0:T(8,128)(2,1)}, u32[]{:S(2)}, u32[]{:S(2)}) collective-permute-start(bf16[36,96,128]{2,1,0:T(8,128)(2,1)} %bitcast.84), channel_id=1, source_target_pairs={{4,0},{8,4},{12,8},{16,12},{20,16},{24,20},{28,24},{32,28},{36,32}... | collective-permute-start | bytes 2654216 | tf_op jit(solution)/shard_map/ppermute | solution.py:12
  12.2 122.4 %collective-permute-start.5 = (bf16[36,96,128]{2,1,0:T(8,128)(2,1)}, bf16[36,96,128]{2,1,0:T(8,128)(2,1)}, u32[]{:S(2)}, u32[]{:S(2)}) collective-permute-start(bf16[36,96,128]{2,1,0:T(8,128)(2,1)} %bitcast.85), channel_id=1, source_target_pairs={{0,16},{4,20},{8,24},{12,28},{16,32},{20,36},{24,40},{28,44},{32,4... | collective-permute-start | bytes 2654216 | tf_op jit(solution)/shard_map/ppermute | solution.py:12
  18.4 118.3 %collective-permute-start.7 = (bf16[36,96,128]{2,1,0:T(8,128)(2,1)}, bf16[36,96,128]{2,1,0:T(8,128)(2,1)}, u32[]{:S(2)}, u32[]{:S(2)}) collective-permute-start(bf16[36,96,128]{2,1,0:T(8,128)(2,1)} %bitcast.86), channel_id=1, source_target_pairs={{16,0},{20,4},{24,8},{28,12},{32,16},{36,20},{40,24},{44,28},{48,3... | collective-permute-start | bytes 2654216 | tf_op jit(solution)/shard_map/ppermute | solution.py:12
  20.5 92.4 %collective-permute-start = (s32[6]{0:T(128)S(1)}, s32[6]{0:T(128)S(1)}, u32[]{:S(2)}, u32[]{:S(2)}) collective-permute-start(s32[6]{0:T(128)S(1)} %get-tuple-element.11), channel_id=1, source_target_pairs={{0,4},{4,8},{8,12},{12,16},{16,20},{20,24},{24,28},{28,32},{32,36}... | collective-permute-start | bytes 80 | tf_op jit(solution)/shard_map/ppermute | solution.py:12
  112.9 3.8 %collective-permute-start.2 = (s32[6]{0:T(128)S(1)}, s32[6]{0:T(128)S(1)}, u32[]{:S(2)}, u32[]{:S(2)}) collective-permute-start(s32[6]{0:T(128)S(1)} %get-tuple-element.10), channel_id=1, source_target_pairs={{4,0},{8,4},{12,8},{16,12},{20,16},{24,20},{28,24},{32,28},{36,32}... | collective-permute-start | bytes 80 | tf_op jit(solution)/shard_map/ppermute | solution.py:12
  116.8 7.7 %collective-permute-start.4 = (s32[6]{0:T(128)S(1)}, s32[6]{0:T(128)S(1)}, u32[]{:S(2)}, u32[]{:S(2)}) collective-permute-start(s32[6]{0:T(128)S(1)} %get-tuple-element.12), channel_id=1, source_target_pairs={{0,16},{4,20},{8,24},{12,28},{16,32},{20,36},{24,40},{28,44},{32,4... | collective-permute-start | bytes 80 | tf_op jit(solution)/shard_map/ppermute | solution.py:12
  124.5 6.6 %collective-permute-start.6 = (s32[6]{0:T(128)S(1)}, s32[6]{0:T(128)S(1)}, u32[]{:S(2)}, u32[]{:S(2)}) collective-permute-start(s32[6]{0:T(128)S(1)} %get-tuple-element.9), channel_id=1, source_target_pairs={{16,0},{20,4},{24,8},{28,12},{32,16},{36,20},{40,24},{44,28},{48,3... | collective-permute-start | bytes 80 | tf_op jit(solution)/shard_map/ppermute | solution.py:12
  139.8 127.3 %all-gather.6.cloned.1.call-start = ((), (), s32[]{:S(2)}) async-start(), calls=%async_computation.1 | async-start | bytes 1474560 | tf_op jit(solution)/shard_map/all_gather | solution.py:74
  146.6 7.6 %copy-start.3 = (f32[6,128]{0,1:T(8,128)S(1)}, f32[6,128]{0,1:T(8,128)}, u32[]{:S(2)}) copy-start(f32[6,128]{0,1:T(8,128)} %convert_reduce_fusion) | copy-start | bytes 9220
  146.6 8.2 %copy-start.2 = (f32[18,128]{0,1:T(8,128)S(1)}, f32[18,128]{0,1:T(8,128)}, u32[]{:S(2)}) copy-start(f32[18,128]{0,1:T(8,128)} %convert_reduce_fusion.1) | copy-start | bytes 27652
  146.6 90.9 %copy-start.5 = (s32[1,1,6,8]{3,1,2,0:T(1,128)S(1)}, s32[1,1,6,8]{3,1,2,0:T(1,128)}, u32[]{:S(2)}) copy-start(s32[1,1,6,8]{3,1,2,0:T(1,128)} %param.11) | copy-start | bytes 580
  240.7 2.7 copy-start.4
  267.1 2.0 copy-start.1
Sparse Core Ops, SparseCore 0:
  140.0 56.5 all-reduce.2
  243.5 21.3 all-gather.5
where the time goes:
time: 279 us; the launch traced here: 277 us
  blocking collectives  102 us (37%)
  local copies, waits for them, and re-layouts  84.6 us (30%)
  other arithmetic  31.2 us (11%)
  starting transfers between devices  25.9 us (9%)
  between operations  17.6 us (6%)
  waiting for transfers between devices  8.44 us (3%)
  matrix products  7.64 us (3%)
    pmax x1, blocking collectives, on_device(): global_bound = lax.pmax(local_bound, ('dom', 'grp'))  80.8 us
    unnamed x19, local copies, waits for them, and re-layouts  54.2 us
    ppermute x8, starting transfers between devices, from_behind(): lax.ppermute(value, axis, [(source, source + steps) for source in range(i...  25.9 us
    reduce_sum x2, other arithmetic, row_bound(): abs_sums = jnp.sum(jnp.abs(tiles), axis=(1, 3), dtype=jnp.float32)  24.1 us
    all_gather x1, blocking collectives, on_device(): lax.all_gather(guest_diag[None], 'grp', axis=0, tiled=True)  11.9 us
    squeeze x2, local copies, waits for them, and re-layouts, row_bound(): diagonal = jnp.diagonal(tiles[:, 0], axis1=1, axis2=2).astype(jnp.float32)  9.6 us
    unnamed x1, blocking collectives  8.91 us
    ppermute x8, waiting for transfers between devices, from_behind(): lax.ppermute(value, axis, [(source, source + steps) for source in range(i...  8.37 us
  transfers between devices with their start and end apart: 10, of which 3 were waited for; matrix products, arithmetic and copies ran while one was open for 40% of the time, Pallas kernels for 0%

commit v1 on v0

v1 whole, which is shorter than its diff:
```python
import jax
import jax.numpy as jnp
from jax import lax
from jax.experimental import pallas as pl
from jax.experimental.pallas import tpu as pltpu
from jax.sharding import PartitionSpec as P

MESH = pl.DeviceIdType.MESH
DOM, GRP, PW = 64, 4, 4
Z, Y, CORES = 8, 4, 2
OFFSETS = (1, -1, PW, -PW)
K = 8
UNIT = 6
RCAP = 36
STORE = 18
PC, TB = 96, 128
OWN = RCAP // 2
GHOSTS = len(OFFSETS) * UNIT
SLOTS = OWN + GHOSTS // 2
LAG = 6
STEPS = SLOTS + 2 * LAG
LOADS = 6
ROUNDS = (GRP - 1, Y * CORES - 1, 4, 4)
F32, BF16 = jnp.float32, jnp.bfloat16


def x_peers(p, g):
    return [(p, lax.rem(g + step, GRP)) for step in range(1, GRP)]


def ghost_peers(p, g):
    return [(lax.rem(p + DOM + offset, DOM), g) for offset in OFFSETS]


def plane_peers(p, g):
    core, z, y = lax.rem(p, CORES), lax.rem(lax.div(p, CORES), Z), lax.div(p, CORES * Z)
    return [
        ((lax.rem(y + dy, Y) * Z + z) * CORES + lax.rem(core + dc, CORES), g)
        for dy in range(Y)
        for dc in range(CORES)
        if dy + dc
    ]


def z_peers(p, g):
    core, z, y = lax.rem(p, CORES), lax.rem(lax.div(p, CORES), Z), lax.div(p, CORES * Z)
    return [((y * Z + lax.rem(z + dz, Z)) * CORES + core, g) for dz in (1, Z - 1, 2, Z - 2)]


def remote(source, target, send, recv, device):
    return pltpu.make_async_remote_copy(
        src_ref=source, dst_ref=target, send_sem=send, recv_sem=recv, device_id=device, device_id_type=MESH
    )


def eye():
    return lax.broadcasted_iota(jnp.int32, (TB, TB), 0) == lax.broadcasted_iota(jnp.int32, (TB, TB), 1)


def bound_row(tiles, row, live, top):
    first = tiles[row, 0].astype(F32)
    total = jnp.abs(first)
    for slot in range(1, K):
        total += jnp.abs(tiles[row, slot].astype(F32))
    sums = jnp.sum(total, axis=1, keepdims=True)
    diagonal = jnp.sum(jnp.where(eye(), first, 0.0), axis=1, keepdims=True)
    ratio = sums / jnp.where(live, diagonal, 1.0)
    return jnp.maximum(top, jnp.where(live, ratio, 0.0))


def inverse_diagonal(tiles, row, live):
    diagonal = jnp.sum(jnp.where(eye(), tiles[row, 0].astype(F32), 0.0), axis=0, keepdims=True)
    return 1.0 / jnp.where(live, diagonal, 1.0)


def product(source, names, tiles, row):
    left = jnp.concatenate([source[name] for name in names], axis=1)
    right = jnp.concatenate([tiles[row, slot] for slot in range(K)], axis=1)
    return lax.dot_general(left, right, (((1,), (1,)), ((), ())), preferred_element_type=F32)


def kernel(
    a_hbm, cols, s_hbm, s_cols, hosts, counts, send_ids, p0_hbm, out_hbm,
    a_v, s_v, p_v, ext, picks, moved, got, prods, inverses, outs, guest, back, name_out, names, mine, heard,
    load_sem, move_send, move_recv, ghost_send, ghost_recv, name_send, name_recv, bound_send, bound_recv,
    back_send, back_recv,
):
    p, g = lax.axis_index("dom"), lax.axis_index("grp")
    xs, ghosts, planes, zs = x_peers(p, g), ghost_peers(p, g), plane_peers(p, g), z_peers(p, g)
    right, left = xs[0], xs[-1]

    barrier = pltpu.get_barrier_semaphore()
    greeted = xs + ghosts + planes + zs
    for device in greeted:
        pl.semaphore_signal(barrier, inc=1, device_id=device, device_id_type=MESH)

    p0_copy = pltpu.make_async_copy(p0_hbm.at[0, 0], p_v, load_sem.at[0])
    ext_copy = pltpu.make_async_copy(p0_hbm.at[0, 0], ext.at[pl.ds(0, RCAP)], load_sem.at[1])
    s_copy = pltpu.make_async_copy(s_hbm.at[0, 0], s_v, load_sem.at[2])
    part = STORE // LOADS
    a_copies = [
        pltpu.make_async_copy(
            a_hbm.at[0, 0, pl.ds(i * part, part)], a_v.at[pl.ds(i * part, part)], load_sem.at[3 + i]
        )
        for i in range(LOADS)
    ]
    for copy in (p0_copy, ext_copy, s_copy, *a_copies):
        copy.start()

    block, rows = hosts[0, 0], counts[0, 0]
    heavy = block < 0
    name_out[...] = jnp.full(name_out.shape, block, jnp.int32)

    p0_copy.wait()
    for j in range(len(OFFSETS)):

        def pick(s, carry, j=j):
            picks[j * UNIT + s] = p_v[jnp.maximum(send_ids[0, 0, j, s], 0)]
            return carry

        lax.fori_loop(0, UNIT, pick, 0)
    ext_copy.wait()

    pl.semaphore_wait(barrier, len(greeted))

    ghost_copies = [
        remote(
            picks.at[pl.ds(j * UNIT, UNIT)],
            ext.at[pl.ds(RCAP + j * UNIT, UNIT)],
            ghost_send.at[j],
            ghost_recv.at[j],
            ghosts[j],
        )
        for j in range(len(OFFSETS))
    ]

    def step_copy(way, t, source):
        return remote(
            source,
            got.at[way * STEPS + t],
            move_send.at[way * STEPS + t],
            move_recv.at[way * STEPS + t],
            (right, left)[way],
        )

    def send_own(t):
        for way in range(2):
            step_copy(way, t, ext.at[way * OWN + t]).start()

    def await_step(t):
        for way in range(2):
            step_copy(way, t, got.at[way * STEPS + t]).wait_recv()

    def send_selected(t, base):
        await_step(t - LAG)
        for way in range(2):
            slot = way * SLOTS + t
            moved[slot] = jnp.where(heavy, ext[base[way] + t], got[way * STEPS + t - LAG])
            step_copy(way, t, moved.at[slot]).start()

    def send_forward(t):
        await_step(t - LAG)
        for way in range(2):
            step_copy(way, t, got.at[way * STEPS + t - LAG]).start()

    for t in range(LAG):
        send_own(t)
        if t < len(OFFSETS):
            ghost_copies[t].start()
    name_copies = [
        remote(name_out, names.at[i], name_send.at[i], name_recv.at[i], xs[i]) for i in range(GRP - 1)
    ]
    for copy in name_copies:
        copy.start()

    own_base = (0, OWN)
    ghost_base = (RCAP - OWN, RCAP + GHOSTS // 2 - OWN)

    own_steps = OWN - LAG
    per_step = (STORE + UNIT) // own_steps
    for i in range(LOADS):
        a_copies[i].wait()
    s_copy.wait()
    top = jnp.zeros((TB, 1), F32)

    def stored_step(i, top):
        send_selected(LAG + i, own_base)
        for n in range(per_step):
            row = i * per_step + n
            top = bound_row(a_v, row, row < rows, top)
        return top

    def surplus_step(i, top):
        send_selected(LAG + STORE // per_step + i, own_base)
        for n in range(per_step):
            top = bound_row(s_v, i * per_step + n, block >= 0, top)
        return top

    top = lax.fori_loop(0, STORE // per_step, stored_step, top)
    top = lax.fori_loop(0, UNIT // per_step, surplus_step, top)
    mine[0] = jnp.broadcast_to(jnp.max(top, axis=0, keepdims=True), (8, TB))

    def bound_copies(k):
        base = sum(ROUNDS[:k])
        peers = (xs, planes, zs, zs)[k]
        return [
            remote(mine.at[k], heard.at[base + i], bound_send.at[base + i], bound_recv.at[base + i], peers[i])
            for i in range(ROUNDS[k])
        ]

    def tell(k):
        for copy in bound_copies(k):
            copy.start()

    def hear(k):
        base = sum(ROUNDS[:k])
        for copy in bound_copies(k):
            copy.wait_recv()
        best = mine[k]
        for i in range(ROUNDS[k]):
            best = jnp.maximum(best, heard[base + i])
        mine[k + 1] = best

    tell(0)
    for copy in ghost_copies:
        copy.wait_recv()

    def own_product(row):
        prods[row] = product(ext, [cols[0, 0, row, slot] for slot in range(K)], a_v, row)
        inverses[row] = jnp.broadcast_to(inverse_diagonal(a_v, row, row < rows), (8, TB))

    third = STORE // 3

    def ghost_step(i, carry):
        send_selected(OWN + i, ghost_base)
        own_product(i)
        return carry

    def forward_step(i, carry):
        send_forward(SLOTS + i)
        own_product(2 * third + i)
        return carry

    def last_step(i, carry):
        send_forward(SLOTS + i)
        return carry

    lax.fori_loop(0, third, ghost_step, 0)
    hear(0)
    tell(1)
    lax.fori_loop(third, 2 * third, ghost_step, 0)
    hear(1)
    tell(2)
    lax.fori_loop(0, third, forward_step, 0)
    hear(2)
    tell(3)
    lax.fori_loop(third, 2 * LAG, last_step, 0)
    hear(3)

    damping = 4.0 / (3.0 * mine[4][0:1, :])

    def finish_own(row, carry):
        value = p_v[row].astype(F32) - damping * inverses[row][0:1, :] * prods[row]
        outs[row] = jnp.where(row < rows, value, 0.0).astype(BF16)
        return carry

    lax.fori_loop(0, STORE, finish_own, 0)
    head_copy = pltpu.make_async_copy(
        outs.at[pl.ds(0, STORE)], out_hbm.at[0, 0, pl.ds(0, STORE)], load_sem.at[0]
    )
    head_copy.start()

    for copy in name_copies:
        copy.wait_recv()
    peer_block = [jnp.max(names[i]) for i in range(GRP - 1)]
    away = jnp.int32(1)
    for i in range(1, GRP - 1):
        away = jnp.where(peer_block[i] < 0, i + 1, away)
    shift = (LAG * (away - 1), STEPS + LAG * (GRP - away - 1))

    def place(name):
        ghost = name >= RCAP
        at = jnp.where(ghost, name - RCAP, name)
        span = jnp.where(ghost, GHOSTS // 2, OWN)
        leftward = at >= span
        t = jnp.where(leftward, at - span, at) + jnp.where(ghost, OWN, 0)
        return t + jnp.where(leftward, shift[1], shift[0])

    lax.fori_loop(STEPS - LAG, STEPS, lambda t, carry: (await_step(t), carry)[1], 0)

    def back_copy(s, i):
        return remote(
            guest.at[s],
            back.at[i, s],
            back_send.at[i * UNIT + s],
            back_recv.at[i * UNIT + s],
            xs[i],
        )

    def guest_step(s, carry):
        places = [place(s_cols[0, 0, s, slot]) for slot in range(K)]
        inverse = inverse_diagonal(s_v, s, block >= 0)
        value = got[places[0]].astype(F32) - damping * inverse * product(got, places, s_v, s)
        guest[s] = value.astype(BF16)
        for i in range(GRP - 1):
            back_copy(s, i).start()
        return carry

    lax.fori_loop(0, UNIT, guest_step, 0)

    def drain(t, carry):
        for way in range(2):
            step_copy(way, t, got.at[way * STEPS + t]).wait_send()
        return carry

    lax.fori_loop(0, STEPS, drain, 0)
    for copy in (*ghost_copies, *name_copies):
        copy.wait_send()
    for k in range(len(ROUNDS)):
        for copy in bound_copies(k):
            copy.wait_send()

    def await_back(s, carry):
        for i in range(GRP - 1):
            back_copy(s, i).wait_recv()
        return carry

    lax.fori_loop(0, UNIT, await_back, 0)
    for b in range((RCAP - STORE) // UNIT):
        holder = jnp.int32(0)
        for i in range(GRP - 1):
            holder = jnp.where(peer_block[i] == b, i, holder)

        def finish_tail(s, carry, b=b, holder=holder):
            outs[STORE + b * UNIT + s] = jnp.where(heavy, back[holder, s], jnp.zeros((PC, TB), BF16))
            return carry

        lax.fori_loop(0, UNIT, finish_tail, 0)
    tail_copy = pltpu.make_async_copy(
        outs.at[pl.ds(STORE, RCAP - STORE)], out_hbm.at[0, 0, pl.ds(STORE, RCAP - STORE)], load_sem.at[1]
    )
    tail_copy.start()

    def drain_back(s, carry):
        for i in range(GRP - 1):
            back_copy(s, i).wait_send()
        return carry

    lax.fori_loop(0, UNIT, drain_back, 0)
    head_copy.wait()
    tail_copy.wait()


def on_device(a_tiles, columns, surplus_tiles, surplus_cols, hosts, counts, send_ids, p0):
    smem, anywhere = pl.BlockSpec(memory_space=pltpu.SMEM), pl.BlockSpec(memory_space=pl.ANY)
    dma = pltpu.SemaphoreType.DMA
    tile = (PC, TB)
    return pl.pallas_call(
        kernel,
        out_shape=jax.ShapeDtypeStruct(p0.shape, p0.dtype),
        in_specs=[anywhere, smem, anywhere, smem, smem, smem, smem, anywhere],
        out_specs=anywhere,
        scratch_shapes=[
            pltpu.VMEM((STORE, K, TB, TB), BF16),
            pltpu.VMEM((UNIT, K, TB, TB), BF16),
            pltpu.VMEM((RCAP, *tile), BF16),
            pltpu.VMEM((RCAP + GHOSTS, *tile), BF16),
            pltpu.VMEM((GHOSTS, *tile), BF16),
            pltpu.VMEM((2 * SLOTS, *tile), BF16),
            pltpu.VMEM((2 * STEPS, *tile), BF16),
            pltpu.VMEM((STORE, *tile), F32),
            pltpu.VMEM((STORE, 8, TB), F32),
            pltpu.VMEM((RCAP, *tile), BF16),
            pltpu.VMEM((UNIT, *tile), BF16),
            pltpu.VMEM((GRP - 1, UNIT, *tile), BF16),
            pltpu.VMEM((8, TB), jnp.int32),
            pltpu.VMEM((GRP - 1, 8, TB), jnp.int32),
            pltpu.VMEM((len(ROUNDS) + 1, 8, TB), F32),
            pltpu.VMEM((sum(ROUNDS), 8, TB), F32),
            dma((3 + LOADS,)),
            dma((2 * STEPS,)),
            dma((2 * STEPS,)),
            dma((len(OFFSETS),)),
            dma((len(OFFSETS),)),
            dma((GRP - 1,)),
            dma((GRP - 1,)),
            dma((sum(ROUNDS),)),
            dma((sum(ROUNDS),)),
            dma(((GRP - 1) * UNIT,)),
            dma(((GRP - 1) * UNIT,)),
        ],
        compiler_params=pltpu.CompilerParams(
            collective_id=0, has_side_effects=True, vmem_limit_bytes=40 * 1024 * 1024
        ),
        cost_estimate=pl.CostEstimate(flops=604_000_000, bytes_accessed=9_000_000, transcendentals=0),
    )(a_tiles, columns, surplus_tiles, surplus_cols, hosts, counts, send_ids, p0)


def solution(mesh):
    in_specs = (
        P("dom", "grp", None, None, None, None),
        P("dom", "grp", None, None),
        P("dom", "grp", None, None, None, None),
        P("dom", "grp", None, None),
        P("dom", "grp"),
        P("dom", "grp"),
        P("dom", "grp", None, None),
        P("dom", "grp", None, None, None),
    )
    out_specs = P("dom", "grp", None, None, None)
    return jax.shard_map(on_device, mesh=mesh, in_specs=in_specs, out_specs=out_specs, check_vma=False)
```

time: 279 us -> 57.6 us (0.21)
  blocking collectives: 102 us -> 0 us
  local copies, waits for them, and re-layouts: 84.6 us -> 7.96 us
  Pallas kernels: 0 us -> 47.5 us
  other arithmetic: 31.2 us -> 0 us
  starting transfers between devices: 25.9 us -> 0 us
  between operations: 17.6 us -> 1.31 us
  waiting for transfers between devices: 8.44 us -> 0 us
  matrix products: 7.64 us -> 0 us
    pmax x1 -> x0, blocking collectives: 80.8 us -> none  [on_device(): global_bound = lax.pmax(local_bound, ('dom', 'grp'))]
    pallas_call x0 -> x1, Pallas kernels: none -> 47.5 us  [on_device(): pl.pallas_call(kernel, out_shape=jax.ShapeDtypeStruct(p0.shape, p0.dtype)...]
    unnamed x19 -> x11, local copies, waits for them, and re-layouts: 54.2 us -> 7.96 us
    ppermute x8 -> x0, starting transfers between devices: 25.9 us -> none  [from_behind(): lax.ppermute(value, axis, [(source, source + steps) for source in range(i...]
    reduce_sum x3 -> x0, other arithmetic: 24.9 us -> none  [the longest x2 24.1 us: row_bound(): abs_sums = jnp.sum(jnp.abs(tiles), axis=(1, 3), dtype=jnp.float32)]
    gather x10 -> x0, local copies, waits for them, and re-layouts: 19.6 us -> none  [the longest x4 6.97 us: on_device(): chosen = neighbour[jnp.clip(their_names, 0, capacity - 1)]]
    all_gather x1 -> x0, blocking collectives: 11.9 us -> none  [on_device(): lax.all_gather(guest_diag[None], 'grp', axis=0, tiled=True)]
    squeeze x3 -> x0, local copies, waits for them, and re-layouts: 10.4 us -> none  [the longest x2 9.6 us: row_bound(): diagonal = jnp.diagonal(tiles[:, 0], axis1=1, axis2=2).astype(jnp.float32)]
  transfers between devices with their start and end apart: 10 -> 0, of which waited for: 3 -> 0; matrix products, arithmetic and copies ran while one was open for 40% -> 0% of each run, Pallas kernels for 0% -> 0%
where the time goes in v1:
time: 57.6 us; the launch traced here: 56.8 us
  Pallas kernels  47.5 us (82%)
  local copies, waits for them, and re-layouts  7.96 us (14%)
  between operations  1.31 us (2%)
    pallas_call x1, Pallas kernels, on_device(): pl.pallas_call(kernel, out_shape=jax.ShapeDtypeStruct(p0.shape, p0.dtype)...  47.5 us
    unnamed x11, local copies, waits for them, and re-layouts  7.96 us

profile of v1, /device:TPU:32, one launch (start us, length us, event | category | flops | bytes accessed | tf_op | source)
XLA Modules:
  0.0 56.8 jit_solution(10567951462365297830)
XLA Ops:
  1.3 0.7 %copy.10.s_cols = s32[1,1,6,8]{3,2,1,0:T(8,128)S(1)} copy(s32[1,1,6,8]{3,1,2,0:T(1,128)} %param.11) | data formatting | bytes 384 | tf_op args[3]
  2.0 0.8 %copy.9.cols = s32[1,1,18,8]{3,2,1,0:T(8,128)S(1)} copy(s32[1,1,18,8]{2,3,1,0:T(8,128)} %param.9) | data formatting | bytes 1152 | tf_op args[1]
  2.8 0.0 copy-start
  2.8 2.3 %copy-done = bf16[1,1,18,8,128,128]{5,4,3,2,1,0:T(8,128)(2,1)S(1)} copy-done((bf16[1,1,18,8,128,128]{5,4,3,2,1,0:T(8,128)(2,1)S(1)}, bf16[1,1,18,8,128,128]{5,4,3,2,1,0:T(8,128)(2,1)}, u32[]{:S(2)}) %copy-start) | copy-done | bytes 4718616
  5.1 0.0 copy-start.1
  5.1 1.4 %copy-done.1 = bf16[1,1,6,8,128,128]{5,4,3,2,1,0:T(8,128)(2,1)S(1)} copy-done((bf16[1,1,6,8,128,128]{5,4,3,2,1,0:T(8,128)(2,1)S(1)}, bf16[1,1,6,8,128,128]{5,4,3,2,1,0:T(8,128)(2,1)}, u32[]{:S(2)}) %copy-start.1) | copy-done | bytes 1572888
  6.5 0.0 copy-start.2
  6.5 1.2 %copy-done.2 = bf16[1,1,36,96,128]{4,3,2,1,0:T(8,128)(2,1)S(1)} copy-done((bf16[1,1,36,96,128]{4,3,2,1,0:T(8,128)(2,1)S(1)}, bf16[1,1,36,96,128]{4,3,2,1,0:T(8,128)(2,1)}, u32[]{:S(2)}) %copy-start.2) | copy-done | bytes 884760
  7.7 0.0 copy-start.3
  7.7 0.7 %copy-done.3 = s32[1,1,4,6]{3,2,1,0:T(4,128)S(1)} copy-done((s32[1,1,4,6]{3,2,1,0:T(4,128)S(1)}, s32[1,1,4,6]{3,2,1,0:T(4,128)}, u32[]{:S(2)}) %copy-start.3) | copy-done | bytes 120
  8.4 47.5 %shard_map.82 = bf16[1,1,36,96,128]{4,3,2,1,0:T(8,128)(2,1)S(1)} custom-call(bf16[1,1,18,8,128,128]{5,4,3,2,1,0:T(8,128)(2,1)S(1)} %copy-done, s32[1,1,18,8]{3,2,1,0:T(8,128)S(1)} %copy.9.cols, bf16[1,1,6,8,128,128]{5,4,3,2,1,0:T(8,128)(2,1)S(1)} %copy-done.1, s32[1,1,6,8]{3,2,1,0:T(8,128)S(1)} %copy.10.s_cols, s32[1,1]{1,0:T(1,128)S(6)} %copy.12.hosts, ...), custom_call_target="tpu_custom_call" | custom-call | flops 604000000 | bytes 9000000 | tf_op jit(solution)/shard_map/pallas_call | solution.py:358
  55.8 0.9 %copy.14 = bf16[1,1,36,96,128]{4,3,2,1,0:T(8,128)(2,1)} copy(bf16[1,1,36,96,128]{4,3,2,1,0:T(8,128)(2,1)S(1)} %shard_map.82) | data formatting | bytes 1769472
Async XLA Ops:
  2.8 2.3 %copy-start = (bf16[1,1,18,8,128,128]{5,4,3,2,1,0:T(8,128)(2,1)S(1)}, bf16[1,1,18,8,128,128]{5,4,3,2,1,0:T(8,128)(2,1)}, u32[]{:S(2)}) copy-start(bf16[1,1,18,8,128,128]{5,4,3,2,1,0:T(8,128)(2,1)} %a_hbm.1) | copy-start | bytes 14155780
  5.1 1.4 %copy-start.1 = (bf16[1,1,6,8,128,128]{5,4,3,2,1,0:T(8,128)(2,1)S(1)}, bf16[1,1,6,8,128,128]{5,4,3,2,1,0:T(8,128)(2,1)}, u32[]{:S(2)}) copy-start(bf16[1,1,6,8,128,128]{5,4,3,2,1,0:T(8,128)(2,1)} %s_hbm.1) | copy-start | bytes 4718596
  6.5 1.2 %copy-start.2 = (bf16[1,1,36,96,128]{4,3,2,1,0:T(8,128)(2,1)S(1)}, bf16[1,1,36,96,128]{4,3,2,1,0:T(8,128)(2,1)}, u32[]{:S(2)}) copy-start(bf16[1,1,36,96,128]{4,3,2,1,0:T(8,128)(2,1)} %p0_hbm.1) | copy-start | bytes 2654212
  7.7 0.7 %copy-start.3 = (s32[1,1,4,6]{3,2,1,0:T(4,128)S(1)}, s32[1,1,4,6]{3,2,1,0:T(4,128)}, u32[]{:S(2)}) copy-start(s32[1,1,4,6]{3,2,1,0:T(4,128)} %send_ids.1) | copy-start | bytes 292

commit v2 on v1

v2 whole, which is shorter than its diff:
```python
import jax
import jax.numpy as jnp
from jax import lax
from jax.experimental import pallas as pl
from jax.experimental.pallas import tpu as pltpu
from jax.sharding import PartitionSpec as P

MESH = pl.DeviceIdType.MESH
DOM, GRP, PW = 64, 4, 4
Z, Y, CORES = 8, 4, 2
OFFSETS = (1, -1, PW, -PW)
K = 8
UNIT = 6
RCAP = 36
STORE = 18
PC, TB = 96, 128
OWN = RCAP // 2
ONE_WAY = OWN + 3 * UNIT // 2
SLOTS = ONE_WAY + UNIT
GHOSTS_AT = (
    ((OWN, UNIT),),
    ((OWN + UNIT, UNIT // 2), (ONE_WAY + OWN, UNIT // 2)),
    ((2 * ONE_WAY, UNIT),),
    ((ONE_WAY + OWN + UNIT // 2, UNIT),),
)
LAG = 7
STEPS = max(ONE_WAY + 2 * LAG, SLOTS + LAG)
LOADS = 6
ROUNDS = (GRP - 1, Y * CORES - 1, 4, 4)
ANSWER_AT, HEAR_AT = (9, None, 12, 17), (13, 20, 32, 41)
VMEM_BYTES = 53 * 1024 * 1024
F32, BF16 = jnp.float32, jnp.bfloat16


def x_peers(p, g):
    return [(p, lax.rem(g + step, GRP)) for step in range(1, GRP)]


def ghost_peers(p, g):
    return [(lax.rem(p + DOM + offset, DOM), g) for offset in OFFSETS]


def linked(p, offset):
    if offset == 1:
        return 1 - lax.div(lax.rem(p, PW), PW - 1)
    if offset == -1:
        return lax.div(lax.rem(p, PW) + PW - 1, PW)
    if offset > 0:
        return 1 - lax.div(p, DOM - PW)
    return lax.div(p + DOM - PW, DOM)


def plane_peers(p, g):
    core, z, y = lax.rem(p, CORES), lax.rem(lax.div(p, CORES), Z), lax.div(p, CORES * Z)
    return [
        ((lax.rem(y + dy, Y) * Z + z) * CORES + lax.rem(core + dc, CORES), g)
        for dy in range(Y)
        for dc in range(CORES)
        if dy + dc
    ]


def z_peers(p, g):
    core, z, y = lax.rem(p, CORES), lax.rem(lax.div(p, CORES), Z), lax.div(p, CORES * Z)
    return [((y * Z + lax.rem(z + dz, Z)) * CORES + core, g) for dz in (1, Z - 1, 2, Z - 2)]


def remote(source, target, send, recv, device):
    return pltpu.make_async_remote_copy(
        src_ref=source, dst_ref=target, send_sem=send, recv_sem=recv, device_id=device, device_id_type=MESH
    )


def eye():
    return lax.broadcasted_iota(jnp.int32, (TB, TB), 0) == lax.broadcasted_iota(jnp.int32, (TB, TB), 1)


def bound_row(tiles, row, live, top):
    first = tiles[row, 0].astype(F32)
    total = jnp.abs(first)
    for slot in range(1, K):
        total += jnp.abs(tiles[row, slot].astype(F32))
    sums = jnp.sum(total, axis=1, keepdims=True)
    diagonal = jnp.sum(jnp.where(eye(), first, 0.0), axis=1, keepdims=True)
    ratio = sums / jnp.where(live, diagonal, 1.0)
    return jnp.maximum(top, jnp.where(live, ratio, 0.0))


def inverse_diagonal(tiles, row, live):
    diagonal = jnp.sum(jnp.where(eye(), tiles[row, 0].astype(F32), 0.0), axis=0, keepdims=True)
    return 1.0 / jnp.where(live, diagonal, 1.0)


def product(source, names, tiles, row):
    left = jnp.concatenate([source[name] for name in names], axis=1)
    right = jnp.concatenate([tiles[row, slot] for slot in range(K)], axis=1)
    return lax.dot_general(left, right, (((1,), (1,)), ((), ())), preferred_element_type=F32)


def position(name):
    shifted = jnp.where(name < RCAP, name + ONE_WAY - OWN, name)
    shifted = jnp.where(name < OWN, name, shifted)
    shifted = jnp.where((name >= RCAP) & (name < 45), name - OWN, shifted)
    shifted = jnp.where((name >= 48) & (name < 54), name + UNIT, shifted)
    return jnp.where(name >= 54, name - UNIT, shifted)


def kernel(
    a_hbm, cols, s_hbm, s_cols, hosts, counts, send_ids, p0_hbm, out,
    a_v, s_v, p_v, ext, picks, moved, got, prods, inverses, guest, back, name_out, names, mine, heard,
    load_sem, move_send, move_recv, ghost_send, ghost_recv, name_send, name_recv, bound_send, bound_recv,
    back_send, back_recv, answer,
):
    p, g = lax.axis_index("dom"), lax.axis_index("grp")
    xs, ghosts, planes, zs = x_peers(p, g), ghost_peers(p, g), plane_peers(p, g), z_peers(p, g)
    right, left = xs[0], xs[-1]

    core, z, y = lax.rem(p, CORES), lax.rem(lax.div(p, CORES), Z), lax.div(p, CORES * Z)
    others = [(ghosts[j], j, linked(p, OFFSETS[j])) for j in range(len(OFFSETS))]
    others += [(device, len(OFFSETS), 1) for device in planes]
    others += [(device, len(OFFSETS) + 1, 1) for device in zs]
    before = []
    for (peer, _), _, there in others:
        peer_core, peer_z, peer_y = lax.rem(peer, CORES), lax.rem(lax.div(peer, CORES), Z), lax.div(peer, CORES * Z)
        mine_is = (z * Y + y) * CORES + core
        before.append((there, lax.div((peer_z * Y + peer_y) * CORES + peer_core + Z * Y * CORES - mine_is, Z * Y * CORES)))
    earlier = [there * is_before for there, is_before in before]
    later = [there * (1 - is_before) for there, is_before in before]
    barrier = pltpu.get_barrier_semaphore()
    for device in xs:
        pl.semaphore_signal(barrier, inc=1, device_id=device, device_id_type=MESH)
    for i, (device, _, _) in enumerate(others):

        @pl.when(earlier[i] == 1)
        def _(device=device):
            pl.semaphore_signal(barrier, inc=1, device_id=device, device_id_type=MESH)

    def load(source, target, i):
        return pltpu.make_async_copy(source, target, load_sem.at[i])

    part = STORE // LOADS
    ext_copies = [
        load(p0_hbm.at[0, 0, pl.ds(way * OWN, OWN)], ext.at[pl.ds(way * ONE_WAY, OWN)], way) for way in range(2)
    ]
    p0_copy = load(p0_hbm.at[0, 0], p_v, 2)
    a_copies = [
        load(a_hbm.at[0, 0, pl.ds(i * part, part)], a_v.at[pl.ds(i * part, part)], 3 + i) for i in range(LOADS)
    ]
    s_copy = load(s_hbm.at[0, 0], s_v, 3 + LOADS)
    for copy in (*ext_copies, p0_copy, *a_copies, s_copy):
        copy.start()

    block, rows = hosts[0, 0], counts[0, 0]
    heavy = block < 0
    name_out[...] = jnp.full(name_out.shape, block, jnp.int32)
    for copy in ext_copies:
        copy.wait()
    pl.semaphore_wait(barrier, GRP - 1 + sum(later))

    def step_copy(way, t, source):
        return remote(
            source,
            got.at[way * STEPS + t],
            move_send.at[way * STEPS + t],
            move_recv.at[way * STEPS + t],
            (right, left)[way],
        )

    def await_step(t):
        for way in range(2):
            step_copy(way, t, got.at[way * STEPS + t]).wait_recv()

    def send_selected(t, base):
        await_step(t - LAG)
        for way in range(2):
            slot = way * SLOTS + t
            moved[slot] = jnp.where(heavy, ext[base[way] + t], got[way * STEPS + t - LAG])
            step_copy(way, t, moved.at[slot]).start()

    def send_forward(t):
        await_step(t - LAG)
        for way in range(2):
            step_copy(way, t, got.at[way * STEPS + t - LAG]).start()

    def one_way(t):
        send_selected(t, (0, ONE_WAY))

    def both_ways(t):
        send_selected(t, (ONE_WAY, ONE_WAY))

    def slots(send, start, end, work=None):
        def step(t, carry):
            send(t)
            if work is not None:
                work(t)
            return carry

        lax.fori_loop(start, end, step, 0)

    for t in range(LAG):
        for way in range(2):
            step_copy(way, t, ext.at[way * ONE_WAY + t]).start()
    name_copies = [
        remote(name_out, names.at[i], name_send.at[i], name_recv.at[i], xs[i]) for i in range(GRP - 1)
    ]
    for copy in name_copies:
        copy.start()

    for i, (device, kind, _) in enumerate(others):
        kind = kind ^ 1 if kind < len(OFFSETS) else kind

        @pl.when(later[i] == 1)
        def _(device=device, kind=kind):
            pl.semaphore_signal(answer.at[kind], inc=1, device_id=device, device_id_type=MESH)

    p0_copy.wait()
    for j in range(len(OFFSETS)):
        for s in range(UNIT):
            picks[j * UNIT + s] = p_v[jnp.maximum(send_ids[0, 0, j, s], 0)]

    def ghost_copy(i, first, count, target, j):
        return remote(
            picks.at[pl.ds(first, count)], ext.at[pl.ds(target, count)], ghost_send.at[i], ghost_recv.at[i], ghosts[j]
        )

    half = UNIT // 2
    ghost_copies = (
        [ghost_copy(0, 0, UNIT, OWN, 0)],
        [ghost_copy(1, UNIT, half, OWN + UNIT, 1), ghost_copy(2, UNIT + half, half, ONE_WAY + OWN, 1)],
        [ghost_copy(3, 2 * UNIT, UNIT, 2 * ONE_WAY, 2)],
        [ghost_copy(4, 3 * UNIT, UNIT, ONE_WAY + OWN + half, 3)],
    )

    for j in (2, 3, 1, 0):

        @pl.when(later[j] == 1)
        def _(j=j):
            for copy in ghost_copies[j]:
                copy.start()

    def await_ghosts(j):
        there = linked(p, -OFFSETS[j])

        @pl.when(there == 1)
        def _():
            for copy in ghost_copies[j]:
                copy.wait_recv()

        @pl.when(there == 0)
        def _():
            for first, count in GHOSTS_AT[j]:
                for s in range(count):
                    ext[first + s] = jnp.zeros((PC, TB), BF16)

    def stored_rows(i, top):
        for n in range(part):
            row = i * part + n
            top = bound_row(a_v, row, row < rows, top)
        return top

    def surplus_rows(i, top):
        for n in range(part):
            top = bound_row(s_v, i * part + n, block >= 0, top)
        return top

    for copy in a_copies:
        copy.wait()
    top = lax.fori_loop(0, LOADS, stored_rows, jnp.zeros((TB, 1), F32))
    s_copy.wait()
    top = lax.fori_loop(0, UNIT // part, surplus_rows, top)
    mine[0] = jnp.broadcast_to(jnp.max(top, axis=0, keepdims=True), (8, TB))

    def bound_copies(k):
        base = sum(ROUNDS[:k])
        peers = (xs, planes, zs, zs)[k]
        return [
            remote(mine.at[k], heard.at[base + i], bound_send.at[base + i], bound_recv.at[base + i], peers[i])
            for i in range(ROUNDS[k])
        ]

    def tell(k):
        if k in (1, 2):
            kind = len(OFFSETS) + k - 1
            answers = sum(n for n, other in zip(earlier, others, strict=True) if other[1] == kind)

            @pl.when(answers > 0)
            def _():
                pl.semaphore_wait(answer.at[kind], answers)

        for copy in bound_copies(k):
            copy.start()

    def hear(k):
        base = sum(ROUNDS[:k])
        for copy in bound_copies(k):
            copy.wait_recv()
        best = mine[k]
        for i in range(ROUNDS[k]):
            best = jnp.maximum(best, heard[base + i])
        mine[k + 1] = best

    def own_product(row):
        names = [position(cols[0, 0, slot, row]) for slot in range(K)]
        prods[row] = product(ext, names, a_v, row)
        inverses[row] = jnp.broadcast_to(inverse_diagonal(a_v, row, row < rows), (8, TB))

    def products(t):
        for n in range(part):
            own_product(part * (t - SLOTS) + n)

    def events(t):
        for j in range(len(OFFSETS)):
            if t == ANSWER_AT[j]:

                @pl.when(earlier[j] == 1)
                def _(j=j):
                    pl.semaphore_wait(answer.at[j], 1)
                    for copy in ghost_copies[j]:
                        copy.start()

        for k in range(len(ROUNDS)):
            if t == HEAR_AT[k]:
                hear(k)
                if k + 1 < len(ROUNDS):
                    tell(k + 1)
        if t == OWN:
            await_ghosts(0)
            await_ghosts(1)
        if t == OWN + half:
            await_ghosts(3)
        if t == ONE_WAY:
            await_ghosts(2)

    tell(0)
    cuts = sorted({LAG, *(t for t in ANSWER_AT if t), *HEAR_AT, OWN, OWN + half, ONE_WAY, SLOTS, SLOTS + LOADS, STEPS})
    cuts = [t for t in cuts if LAG <= t <= STEPS]
    for start, end in zip(cuts, cuts[1:] + [STEPS], strict=True):
        events(start)
        if start < ONE_WAY:
            slots(one_way, start, end)
        elif start < SLOTS:
            slots(both_ways, start, end)
        elif start < STEPS:
            slots(send_forward, start, end, products if start < SLOTS + LOADS else None)

    damping = 4.0 / (3.0 * mine[len(ROUNDS)][0:1, :])
    for row in range(STORE):
        value = p_v[row].astype(F32) - damping * inverses[row][0:1, :] * prods[row]
        out[0, 0, row] = jnp.where(row < rows, value, 0.0).astype(BF16)

    for copy in name_copies:
        copy.wait_recv()
    peer_block = [jnp.max(names[i]) for i in range(GRP - 1)]
    away = jnp.int32(1)
    for i in range(1, GRP - 1):
        away = jnp.where(peer_block[i] < 0, i + 1, away)
    shift = (
        LAG * (away - 1),
        STEPS - ONE_WAY + LAG * (GRP - away - 1),
        jnp.where(away == GRP - 1, STEPS, LAG * (away - 1)) - ONE_WAY,
    )

    def place(name):
        at = position(name)
        return at + jnp.where(at < ONE_WAY, shift[0], jnp.where(at < 2 * ONE_WAY, shift[1], shift[2]))

    def back_copy(n, i):
        rows_of = pl.ds(n * half, half)
        return remote(
            guest.at[rows_of], back.at[i, rows_of], back_send.at[2 * i + n], back_recv.at[2 * i + n], xs[i]
        )

    lax.fori_loop(STEPS - LAG, STEPS, lambda t, carry: (await_step(t), carry)[1], 0)
    for n in range(2):
        for s in range(n * half, (n + 1) * half):
            places = [place(s_cols[0, s, 0, slot]) for slot in range(K)]
            inverse = inverse_diagonal(s_v, s, block >= 0)
            value = got[places[0]].astype(F32) - damping * inverse * product(got, places, s_v, s)
            guest[s] = value.astype(BF16)
        for i in (1, 0, 2):
            back_copy(n, i).start()

    def drain(t, carry):
        for way in range(2):
            step_copy(way, t, got.at[way * STEPS + t]).wait_send()
        return carry

    lax.fori_loop(0, STEPS, drain, 0)
    for copy in name_copies:
        copy.wait_send()
    for j in range(len(OFFSETS)):

        @pl.when(linked(p, OFFSETS[j]) == 1)
        def _(j=j):
            for copy in ghost_copies[j]:
                copy.wait_send()

    for k in range(len(ROUNDS)):
        for copy in bound_copies(k):
            copy.wait_send()

    for n in range(2):
        for i in range(GRP - 1):
            back_copy(n, i).wait_recv()
    for b in range((RCAP - STORE) // UNIT):
        holder = jnp.int32(0)
        for i in range(GRP - 1):
            holder = jnp.where(peer_block[i] == b, i, holder)
        for s in range(UNIT):
            out[0, 0, STORE + b * UNIT + s] = jnp.where(heavy, back[holder, s], jnp.zeros((PC, TB), BF16))
    for n in range(2):
        for i in range(GRP - 1):
            back_copy(n, i).wait_send()


def on_device(a_tiles, columns, surplus_tiles, surplus_cols, hosts, counts, send_ids, p0):
    smem, hbm = pl.BlockSpec(memory_space=pltpu.SMEM), pl.BlockSpec(memory_space=pltpu.HBM)
    dma = pltpu.SemaphoreType.DMA
    tile = (PC, TB)
    return pl.pallas_call(
        kernel,
        out_shape=jax.ShapeDtypeStruct(p0.shape, p0.dtype),
        in_specs=[hbm, smem, hbm, smem, smem, smem, smem, hbm],
        out_specs=pl.BlockSpec(memory_space=pltpu.VMEM),
        scratch_shapes=[
            pltpu.VMEM((STORE, K, TB, TB), BF16),
            pltpu.VMEM((UNIT, K, TB, TB), BF16),
            pltpu.VMEM((RCAP, *tile), BF16),
            pltpu.VMEM((2 * ONE_WAY + UNIT, *tile), BF16),
            pltpu.VMEM((len(OFFSETS) * UNIT, *tile), BF16),
            pltpu.VMEM((2 * SLOTS, *tile), BF16),
            pltpu.VMEM((2 * STEPS, *tile), BF16),
            pltpu.VMEM((STORE, *tile), F32),
            pltpu.VMEM((STORE, 8, TB), F32),
            pltpu.VMEM((UNIT, *tile), BF16),
            pltpu.VMEM((GRP - 1, UNIT, *tile), BF16),
            pltpu.VMEM((8, TB), jnp.int32),
            pltpu.VMEM((GRP - 1, 8, TB), jnp.int32),
            pltpu.VMEM((len(ROUNDS) + 1, 8, TB), F32),
            pltpu.VMEM((sum(ROUNDS), 8, TB), F32),
            dma((4 + LOADS,)),
            dma((2 * STEPS,)),
            dma((2 * STEPS,)),
            dma((5,)),
            dma((5,)),
            dma((GRP - 1,)),
            dma((GRP - 1,)),
            dma((sum(ROUNDS),)),
            dma((sum(ROUNDS),)),
            dma((2 * (GRP - 1),)),
            dma((2 * (GRP - 1),)),
            pltpu.SemaphoreType.REGULAR((len(OFFSETS) + 2,)),
        ],
        compiler_params=pltpu.CompilerParams(
            collective_id=0, has_side_effects=True, vmem_limit_bytes=VMEM_BYTES
        ),
        cost_estimate=pl.CostEstimate(flops=604_000_000, bytes_accessed=9_000_000, transcendentals=0),
    )(
        a_tiles,
        jnp.transpose(columns, (0, 1, 3, 2)),
        surplus_tiles,
        jnp.transpose(surplus_cols, (0, 2, 1, 3)),
        hosts,
        counts,
        send_ids,
        p0,
    )


def solution(mesh):
    in_specs = (
        P("dom", "grp", None, None, None, None),
        P("dom", "grp", None, None),
        P("dom", "grp", None, None, None, None),
        P("dom", "grp", None, None),
        P("dom", "grp"),
        P("dom", "grp"),
        P("dom", "grp", None, None),
        P("dom", "grp", None, None, None),
    )
    out_specs = P("dom", "grp", None, None, None)
    return jax.shard_map(on_device, mesh=mesh, in_specs=in_specs, out_specs=out_specs, check_vma=False)
```

time: 57.6 us -> 45.2 us (0.78)
  the two profiles are of different devices: /device:TPU:32 before, /device:TPU:8 now
where the time goes in v2:
time: 45.2 us; the launch traced here: 45 us
  Pallas kernels  40.8 us (90%)
  local copies, waits for them, and re-layouts  2.96 us (7%)
  between operations  1.32 us (3%)
    pallas_call x1, Pallas kernels, on_device(): pl.pallas_call(kernel, out_shape=jax.ShapeDtypeStruct(p0.shape, p0.dtype)...  40.8 us
    unnamed x7, local copies, waits for them, and re-layouts  2.96 us

profile of v2, /device:TPU:8, one launch (start us, length us, event | category | flops | bytes accessed | tf_op | source)
XLA Modules:
  0.0 45.0 jit_solution(18345641023464069639)
XLA Ops:
  1.3 0.0 copy-start
  1.3 0.7 %copy-done = s32[1,1,18,8]{2,3,1,0:T(8,128)S(1)} copy-done((s32[1,1,18,8]{2,3,1,0:T(8,128)S(1)}, s32[1,1,18,8]{2,3,1,0:T(8,128)}, u32[]{:S(2)}) %copy-start) | copy-done | bytes 600
  2.0 0.0 copy-start.1
  2.0 0.7 %copy-done.1 = s32[1,1,6,8]{3,1,2,0:T(1,128)S(1)} copy-done((s32[1,1,6,8]{3,1,2,0:T(1,128)S(1)}, s32[1,1,6,8]{3,1,2,0:T(1,128)}, u32[]{:S(2)}) %copy-start.1) | copy-done | bytes 216
  2.7 0.0 copy-start.2
  2.7 0.7 %copy-done.2 = s32[1,1,4,6]{3,2,1,0:T(4,128)S(1)} copy-done((s32[1,1,4,6]{3,2,1,0:T(4,128)S(1)}, s32[1,1,4,6]{3,2,1,0:T(4,128)}, u32[]{:S(2)}) %copy-start.2) | copy-done | bytes 120
  3.4 40.8 %shard_map.82 = bf16[1,1,36,96,128]{4,3,2,1,0:T(8,128)(2,1)S(1)} custom-call(bf16[1,1,18,8,128,128]{5,4,3,2,1,0:T(8,128)(2,1)} %a_hbm.1, s32[1,1,8,18]{3,2,1,0:T(8,128)S(1)} %bitcast.2, bf16[1,1,6,8,128,128]{5,4,3,2,1,0:T(8,128)(2,1)} %s_hbm.1, s32[1,6,1,8]{3,2,1,0:T(1,128)S(1)} %bitcast.3, s32[1,1]{1,0:T(1,128)S(6)} %copy.10.hosts, ...), custom_call_target="tpu_custom_call" | custom-call | flops 604000000 | bytes 9000000 | tf_op jit(solution)/shard_map/pallas_call | solution.py:420
  44.1 0.9 %copy.12 = bf16[1,1,36,96,128]{4,3,2,1,0:T(8,128)(2,1)} copy(bf16[1,1,36,96,128]{4,3,2,1,0:T(8,128)(2,1)S(1)} %shard_map.82) | data formatting | bytes 1769472
Async XLA Ops:
  1.3 0.7 %copy-start = (s32[1,1,18,8]{2,3,1,0:T(8,128)S(1)}, s32[1,1,18,8]{2,3,1,0:T(8,128)}, u32[]{:S(2)}) copy-start(s32[1,1,18,8]{2,3,1,0:T(8,128)} %param.9) | copy-start | bytes 1732
  2.0 0.7 %copy-start.1 = (s32[1,1,6,8]{3,1,2,0:T(1,128)S(1)}, s32[1,1,6,8]{3,1,2,0:T(1,128)}, u32[]{:S(2)}) copy-start(s32[1,1,6,8]{3,1,2,0:T(1,128)} %param.11) | copy-start | bytes 580
  2.7 0.7 %copy-start.2 = (s32[1,1,4,6]{3,2,1,0:T(4,128)S(1)}, s32[1,1,4,6]{3,2,1,0:T(4,128)}, u32[]{:S(2)}) copy-start(s32[1,1,4,6]{3,2,1,0:T(4,128)} %send_ids.1) | copy-start | bytes 292

commit v3 on v2

--- a/solution.py
+++ b/solution.py
@@ -27,8 +27,9 @@
 STEPS = max(ONE_WAY + 2 * LAG, SLOTS + LAG)
 LOADS = 6
 ROUNDS = (GRP - 1, Y * CORES - 1, 4, 4)
-ANSWER_AT, HEAR_AT = (9, None, 12, 17), (13, 20, 32, 41)
-VMEM_BYTES = 53 * 1024 * 1024
+ANSWER_AT, HEAR_AT = (8, None, 10, 15), (13, 23)
+HEAR_Z = ((29, 4, 8), (33, 2, 4), (36, 0, 2))
+VMEM_BYTES = 60 * 1024 * 1024
 F32, BF16 = jnp.float32, jnp.bfloat16
 
 
@@ -106,7 +107,8 @@
 
 
 def kernel(
-    a_hbm, cols, s_hbm, s_cols, hosts, counts, send_ids, p0_hbm, out,
+    a_hbm, cols_hbm, s_hbm, s_cols_hbm, hosts_hbm, counts_hbm, send_ids_hbm, p0_hbm, out_hbm,
+    cols, s_cols, hosts, counts, send_ids, outs,
     a_v, s_v, p_v, ext, picks, moved, got, prods, inverses, guest, back, name_out, names, mine, heard,
     load_sem, move_send, move_recv, ghost_send, ghost_recv, name_send, name_recv, bound_send, bound_recv,
     back_send, back_recv, answer,
@@ -147,9 +149,19 @@
         load(a_hbm.at[0, 0, pl.ds(i * part, part)], a_v.at[pl.ds(i * part, part)], 3 + i) for i in range(LOADS)
     ]
     s_copy = load(s_hbm.at[0, 0], s_v, 3 + LOADS)
-    for copy in (*ext_copies, p0_copy, *a_copies, s_copy):
+    integers = (
+        (hosts_hbm, hosts),
+        (counts_hbm, counts),
+        (send_ids_hbm, send_ids),
+        (cols_hbm, cols),
+        (s_cols_hbm, s_cols),
+    )
+    integer_copies = [load(*pair, 4 + LOADS + i) for i, pair in enumerate(integers)]
+    for copy in (*integer_copies, *ext_copies, p0_copy, *a_copies, s_copy):
         copy.start()
 
+    for copy in integer_copies:
+        copy.wait()
     block, rows = hosts[0, 0], counts[0, 0]
     heavy = block < 0
     name_out[...] = jnp.full(name_out.shape, block, jnp.int32)
@@ -166,20 +178,23 @@
             (right, left)[way],
         )
 
+    def await_way(way, t):
+        step_copy(way, t, got.at[way * STEPS + t]).wait_recv()
+
     def await_step(t):
         for way in range(2):
-            step_copy(way, t, got.at[way * STEPS + t]).wait_recv()
+            await_way(way, t)
 
     def send_selected(t, base):
-        await_step(t - LAG)
         for way in range(2):
+            await_way(way, t - LAG)
             slot = way * SLOTS + t
             moved[slot] = jnp.where(heavy, ext[base[way] + t], got[way * STEPS + t - LAG])
             step_copy(way, t, moved.at[slot]).start()
 
     def send_forward(t):
-        await_step(t - LAG)
         for way in range(2):
+            await_way(way, t - LAG)
             step_copy(way, t, got.at[way * STEPS + t - LAG]).start()
 
     def one_way(t):
@@ -304,9 +319,12 @@
         prods[row] = product(ext, names, a_v, row)
         inverses[row] = jnp.broadcast_to(inverse_diagonal(a_v, row, row < rows), (8, TB))
 
-    def products(t):
-        for n in range(part):
-            own_product(part * (t - SLOTS) + n)
+    def one_product(t):
+        own_product(t - ONE_WAY)
+
+    def two_products(t):
+        for n in range(2):
+            own_product(UNIT + 2 * (t - SLOTS) + n)
 
     def events(t):
         for j in range(len(OFFSETS)):
@@ -318,11 +336,18 @@
                     for copy in ghost_copies[j]:
                         copy.start()
 
-        for k in range(len(ROUNDS)):
+        for k in range(2):
             if t == HEAR_AT[k]:
                 hear(k)
-                if k + 1 < len(ROUNDS):
-                    tell(k + 1)
+                tell(k + 1)
+        for at, first, last in HEAR_Z:
+            if t == at:
+
+                @pl.when((z >= first) & (z < last))
+                def _():
+                    hear(2)
+                    tell(3)
+
         if t == OWN:
             await_ghosts(0)
             await_ghosts(1)
@@ -332,21 +357,24 @@
             await_ghosts(2)
 
     tell(0)
-    cuts = sorted({LAG, *(t for t in ANSWER_AT if t), *HEAR_AT, OWN, OWN + half, ONE_WAY, SLOTS, SLOTS + LOADS, STEPS})
+    cuts = sorted({LAG, *(t for t in ANSWER_AT if t), *HEAR_AT, *(at for at, _, _ in HEAR_Z), OWN, OWN + half, ONE_WAY, SLOTS, SLOTS + UNIT, STEPS})
     cuts = [t for t in cuts if LAG <= t <= STEPS]
     for start, end in zip(cuts, cuts[1:] + [STEPS], strict=True):
         events(start)
         if start < ONE_WAY:
             slots(one_way, start, end)
         elif start < SLOTS:
-            slots(both_ways, start, end)
+            slots(both_ways, start, end, one_product)
         elif start < STEPS:
-            slots(send_forward, start, end, products if start < SLOTS + LOADS else None)
-
+            slots(send_forward, start, end, two_products if start < SLOTS + UNIT else None)
+
+    hear(3)
     damping = 4.0 / (3.0 * mine[len(ROUNDS)][0:1, :])
     for row in range(STORE):
         value = p_v[row].astype(F32) - damping * inverses[row][0:1, :] * prods[row]
-        out[0, 0, row] = jnp.where(row < rows, value, 0.0).astype(BF16)
+        outs[row] = jnp.where(row < rows, value, 0.0).astype(BF16)
+    head_copy = load(outs.at[pl.ds(0, STORE)], out_hbm.at[0, 0, pl.ds(0, STORE)], 0)
+    head_copy.start()
 
     for copy in name_copies:
         copy.wait_recv()
@@ -407,22 +435,46 @@
         for i in range(GRP - 1):
             holder = jnp.where(peer_block[i] == b, i, holder)
         for s in range(UNIT):
-            out[0, 0, STORE + b * UNIT + s] = jnp.where(heavy, back[holder, s], jnp.zeros((PC, TB), BF16))
+            outs[STORE + b * UNIT + s] = jnp.where(heavy, back[holder, s], jnp.zeros((PC, TB), BF16))
+    tail_copy = load(outs.at[pl.ds(STORE, RCAP - STORE)], out_hbm.at[0, 0, pl.ds(STORE, RCAP - STORE)], 1)
+    tail_copy.start()
     for n in range(2):
         for i in range(GRP - 1):
             back_copy(n, i).wait_send()
+    head_copy.wait()
+    tail_copy.wait()
+
+
+def hand_over(source, target, held, sem):
+    part = RCAP // 2
+    rows_of = [pl.ds(i * part, part) for i in range(2)]
+    loads = [pltpu.make_async_copy(source.at[0, 0, r], held.at[r], sem.at[i]) for i, r in enumerate(rows_of)]
+    stores = [pltpu.make_async_copy(held.at[r], target.at[0, 0, r], sem.at[2 + i]) for i, r in enumerate(rows_of)]
+    for copy in loads:
+        copy.start()
+    for load, store in zip(loads, stores, strict=True):
+        load.wait()
+        store.start()
+    for copy in stores:
+        copy.wait()
 
 
 def on_device(a_tiles, columns, surplus_tiles, surplus_cols, hosts, counts, send_ids, p0):
-    smem, hbm = pl.BlockSpec(memory_space=pltpu.SMEM), pl.BlockSpec(memory_space=pltpu.HBM)
+    hbm = pl.BlockSpec(memory_space=pltpu.HBM)
     dma = pltpu.SemaphoreType.DMA
     tile = (PC, TB)
-    return pl.pallas_call(
+    smoothed = pl.pallas_call(
         kernel,
         out_shape=jax.ShapeDtypeStruct(p0.shape, p0.dtype),
-        in_specs=[hbm, smem, hbm, smem, smem, smem, smem, hbm],
-        out_specs=pl.BlockSpec(memory_space=pltpu.VMEM),
+        in_specs=[hbm] * 8,
+        out_specs=hbm,
         scratch_shapes=[
+            pltpu.SMEM((1, 1, K, STORE), jnp.int32),
+            pltpu.SMEM((1, UNIT, 1, K), jnp.int32),
+            pltpu.SMEM((1, 1), jnp.int32),
+            pltpu.SMEM((1, 1), jnp.int32),
+            pltpu.SMEM((1, 1, len(OFFSETS), UNIT), jnp.int32),
+            pltpu.VMEM((RCAP, *tile), BF16),
             pltpu.VMEM((STORE, K, TB, TB), BF16),
             pltpu.VMEM((UNIT, K, TB, TB), BF16),
             pltpu.VMEM((RCAP, *tile), BF16),
@@ -438,7 +490,7 @@
             pltpu.VMEM((GRP - 1, 8, TB), jnp.int32),
             pltpu.VMEM((len(ROUNDS) + 1, 8, TB), F32),
             pltpu.VMEM((sum(ROUNDS), 8, TB), F32),
-            dma((4 + LOADS,)),
+            dma((9 + LOADS,)),
             dma((2 * STEPS,)),
             dma((2 * STEPS,)),
             dma((5,)),
@@ -465,6 +517,14 @@
         send_ids,
         p0,
     )
+    return pl.pallas_call(
+        hand_over,
+        out_shape=jax.ShapeDtypeStruct(p0.shape, p0.dtype),
+        in_specs=[hbm],
+        out_specs=hbm,
+        scratch_shapes=[pltpu.VMEM((RCAP, *tile), BF16), dma((4,))],
+        compiler_params=pltpu.CompilerParams(vmem_limit_bytes=VMEM_BYTES),
+    )(smoothed)
 
 
 def solution(mesh):

time: 45.2 us -> 43 us (0.951)
  the two profiles are of different devices: /device:TPU:8 before, /device:TPU:32 now
where the time goes in v3:
time: 43 us; the launch traced here: 42.5 us
  Pallas kernels  41.2 us (96%)
  between operations  1.3 us (3%)
    pallas_call x1, Pallas kernels, on_device(): pl.pallas_call(kernel, out_shape=jax.ShapeDtypeStruct(p0.shape, p0.dtype)...  39.2 us
    pallas_call x1, Pallas kernels, on_device(): pl.pallas_call(hand_over, out_shape=jax.ShapeDtypeStruct(p0.shape, p0.dty...  1.96 us

profile of v3, /device:TPU:32, one launch (start us, length us, event | category | flops | bytes accessed | tf_op | source)
XLA Modules:
  0.0 42.5 jit_solution(17151738995710885781)
XLA Ops:
  1.3 39.2 %shard_map.82.source = bf16[1,1,36,96,128]{4,3,2,1,0:T(8,128)(2,1)} custom-call(bf16[1,1,18,8,128,128]{5,4,3,2,1,0:T(8,128)(2,1)} %a_hbm.1, s32[1,1,8,18]{3,2,1,0:T(8,128)} %bitcast.2, bf16[1,1,6,8,128,128]{5,4,3,2,1,0:T(8,128)(2,1)} %s_hbm.1, s32[1,6,1,8]{3,2,1,0:T(1,128)} %bitcast.3, s32[1,1]{1,0:T(1,128)S(6)} %copy.9.hosts_hbm, ...), custom_call_target="tpu_custom_call" | custom-call | flops 604000000 | bytes 9000000 | tf_op jit(solution)/shard_map/pallas_call | solution.py:466
  40.6 2.0 %shard_map.83 = bf16[1,1,36,96,128]{4,3,2,1,0:T(8,128)(2,1)} custom-call(bf16[1,1,36,96,128]{4,3,2,1,0:T(8,128)(2,1)} %shard_map.82.source), custom_call_target="tpu_custom_call" | custom-call | tf_op jit(solution)/shard_map/pallas_call | solution.py:520

commit v4 on v3

--- a/solution.py
+++ b/solution.py
@@ -19,16 +19,15 @@
 SLOTS = ONE_WAY + UNIT
 GHOSTS_AT = (
     ((OWN, UNIT),),
-    ((OWN + UNIT, UNIT // 2), (ONE_WAY + OWN, UNIT // 2)),
+    ((ONE_WAY + OWN, UNIT),),
     ((2 * ONE_WAY, UNIT),),
-    ((ONE_WAY + OWN + UNIT // 2, UNIT),),
+    ((OWN + UNIT, UNIT // 2), (ONE_WAY + OWN + UNIT, UNIT // 2)),
 )
-LAG = 7
+LAG = 6
 STEPS = max(ONE_WAY + 2 * LAG, SLOTS + LAG)
 LOADS = 6
-ROUNDS = (GRP - 1, Y * CORES - 1, 4, 4)
-ANSWER_AT, HEAR_AT = (8, None, 10, 15), (13, 23)
-HEAR_Z = ((29, 4, 8), (33, 2, 4), (36, 0, 2))
+ROUNDS = (GRP - 1, Y * CORES - 1, Z - 1)
+ANSWER_AT, HEAR_AT = (8, None, 10, 15), (15, 28)
 VMEM_BYTES = 60 * 1024 * 1024
 F32, BF16 = jnp.float32, jnp.bfloat16
 
@@ -63,7 +62,7 @@
 
 def z_peers(p, g):
     core, z, y = lax.rem(p, CORES), lax.rem(lax.div(p, CORES), Z), lax.div(p, CORES * Z)
-    return [((y * Z + lax.rem(z + dz, Z)) * CORES + core, g) for dz in (1, Z - 1, 2, Z - 2)]
+    return [((y * Z + lax.rem(z + dz, Z)) * CORES + core, g) for dz in range(1, Z)]
 
 
 def remote(source, target, send, recv, device):
@@ -101,9 +100,9 @@
 def position(name):
     shifted = jnp.where(name < RCAP, name + ONE_WAY - OWN, name)
     shifted = jnp.where(name < OWN, name, shifted)
-    shifted = jnp.where((name >= RCAP) & (name < 45), name - OWN, shifted)
-    shifted = jnp.where((name >= 48) & (name < 54), name + UNIT, shifted)
-    return jnp.where(name >= 54, name - UNIT, shifted)
+    for first, move in ((RCAP, -OWN), (42, 3), (48, UNIT), (54, -30), (57, -UNIT)):
+        shifted = jnp.where(name >= first, name + move, shifted)
+    return shifted
 
 
 def kernel(
@@ -167,7 +166,16 @@
     name_out[...] = jnp.full(name_out.shape, block, jnp.int32)
     for copy in ext_copies:
         copy.wait()
+    def say(first, last):
+        for i, (device, kind, _) in list(enumerate(others))[first:last]:
+            kind = kind ^ 1 if kind < len(OFFSETS) else kind
+
+            @pl.when(later[i] == 1)
+            def _(device=device, kind=kind):
+                pl.semaphore_signal(answer.at[kind], inc=1, device_id=device, device_id_type=MESH)
+
     pl.semaphore_wait(barrier, GRP - 1 + sum(later))
+    say(0, len(OFFSETS))
 
     def step_copy(way, t, source):
         return remote(
@@ -221,13 +229,7 @@
     for copy in name_copies:
         copy.start()
 
-    for i, (device, kind, _) in enumerate(others):
-        kind = kind ^ 1 if kind < len(OFFSETS) else kind
-
-        @pl.when(later[i] == 1)
-        def _(device=device, kind=kind):
-            pl.semaphore_signal(answer.at[kind], inc=1, device_id=device, device_id_type=MESH)
-
+    say(len(OFFSETS), len(others))
     p0_copy.wait()
     for j in range(len(OFFSETS)):
         for s in range(UNIT):
@@ -241,12 +243,15 @@
     half = UNIT // 2
     ghost_copies = (
         [ghost_copy(0, 0, UNIT, OWN, 0)],
-        [ghost_copy(1, UNIT, half, OWN + UNIT, 1), ghost_copy(2, UNIT + half, half, ONE_WAY + OWN, 1)],
-        [ghost_copy(3, 2 * UNIT, UNIT, 2 * ONE_WAY, 2)],
-        [ghost_copy(4, 3 * UNIT, UNIT, ONE_WAY + OWN + half, 3)],
+        [ghost_copy(1, UNIT, UNIT, ONE_WAY + OWN, 1)],
+        [ghost_copy(2, 2 * UNIT, UNIT, 2 * ONE_WAY, 2)],
+        [
+            ghost_copy(3, 3 * UNIT, half, OWN + UNIT, 3),
+            ghost_copy(4, 3 * UNIT + half, half, ONE_WAY + OWN + UNIT, 3),
+        ],
     )
 
-    for j in (2, 3, 1, 0):
+    for j in (1, 0, 3, 2):
 
         @pl.when(later[j] == 1)
         def _(j=j):
@@ -287,7 +292,7 @@
 
     def bound_copies(k):
         base = sum(ROUNDS[:k])
-        peers = (xs, planes, zs, zs)[k]
+        peers = (xs, planes, zs)[k]
         return [
             remote(mine.at[k], heard.at[base + i], bound_send.at[base + i], bound_recv.at[base + i], peers[i])
             for i in range(ROUNDS[k])
@@ -340,24 +345,16 @@
             if t == HEAR_AT[k]:
                 hear(k)
                 tell(k + 1)
-        for at, first, last in HEAR_Z:
-            if t == at:
-
-                @pl.when((z >= first) & (z < last))
-                def _():
-                    hear(2)
-                    tell(3)
-
         if t == OWN:
             await_ghosts(0)
             await_ghosts(1)
-        if t == OWN + half:
+        if t == OWN + UNIT:
             await_ghosts(3)
         if t == ONE_WAY:
             await_ghosts(2)
 
     tell(0)
-    cuts = sorted({LAG, *(t for t in ANSWER_AT if t), *HEAR_AT, *(at for at, _, _ in HEAR_Z), OWN, OWN + half, ONE_WAY, SLOTS, SLOTS + UNIT, STEPS})
+    cuts = sorted({LAG, *(t for t in ANSWER_AT if t), *HEAR_AT, OWN, OWN + UNIT, ONE_WAY, SLOTS, SLOTS + UNIT, STEPS})
     cuts = [t for t in cuts if LAG <= t <= STEPS]
     for start, end in zip(cuts, cuts[1:] + [STEPS], strict=True):
         events(start)
@@ -368,7 +365,7 @@
         elif start < STEPS:
             slots(send_forward, start, end, two_products if start < SLOTS + UNIT else None)
 
-    hear(3)
+    hear(2)
     damping = 4.0 / (3.0 * mine[len(ROUNDS)][0:1, :])
     for row in range(STORE):
         value = p_v[row].astype(F32) - damping * inverses[row][0:1, :] * prods[row]

time: 43 us -> 41.9 us (0.974)
  Pallas kernels: 41.2 us -> 40.2 us
    pallas_call x1, Pallas kernels: 39.2 us -> 38.3 us  [on_device(): pl.pallas_call(kernel, out_shape=jax.ShapeDtypeStruct(p0.shape, p0.dtype)...]
where the time goes in v4:
time: 41.9 us; the launch traced here: 41.5 us
  Pallas kernels  40.2 us (96%)
  between operations  1.3 us (3%)
    pallas_call x1, Pallas kernels, on_device(): pl.pallas_call(kernel, out_shape=jax.ShapeDtypeStruct(p0.shape, p0.dtype)...  38.3 us
    pallas_call x1, Pallas kernels, on_device(): pl.pallas_call(hand_over, out_shape=jax.ShapeDtypeStruct(p0.shape, p0.dty...  1.96 us

profile of v4, /device:TPU:32, one launch (start us, length us, event | category | flops | bytes accessed | tf_op | source)
XLA Modules:
  0.0 41.5 jit_solution(2211851624010228158)
XLA Ops:
  1.3 38.3 %shard_map.82.source = bf16[1,1,36,96,128]{4,3,2,1,0:T(8,128)(2,1)} custom-call(bf16[1,1,18,8,128,128]{5,4,3,2,1,0:T(8,128)(2,1)} %a_hbm.1, s32[1,1,8,18]{3,2,1,0:T(8,128)} %bitcast.2, bf16[1,1,6,8,128,128]{5,4,3,2,1,0:T(8,128)(2,1)} %s_hbm.1, s32[1,6,1,8]{3,2,1,0:T(1,128)} %bitcast.3, s32[1,1]{1,0:T(1,128)S(6)} %copy.9.hosts_hbm, ...), custom_call_target="tpu_custom_call" | custom-call | flops 604000000 | bytes 9000000 | tf_op jit(solution)/shard_map/pallas_call | solution.py:463
  39.6 2.0 %shard_map.83 = bf16[1,1,36,96,128]{4,3,2,1,0:T(8,128)(2,1)} custom-call(bf16[1,1,36,96,128]{4,3,2,1,0:T(8,128)(2,1)} %shard_map.82.source), custom_call_target="tpu_custom_call" | custom-call | tf_op jit(solution)/shard_map/pallas_call | solution.py:517

commit v5 on v4

--- a/solution.py
+++ b/solution.py
@@ -108,7 +108,7 @@
 def kernel(
     a_hbm, cols_hbm, s_hbm, s_cols_hbm, hosts_hbm, counts_hbm, send_ids_hbm, p0_hbm, out_hbm,
     cols, s_cols, hosts, counts, send_ids, outs,
-    a_v, s_v, p_v, ext, picks, moved, got, prods, inverses, guest, back, name_out, names, mine, heard,
+    a_v, s_v, p_v, ext, picks, moved, got, prods, inverses, guest, back_first, back_second, name_out, names, mine, heard,
     load_sem, move_send, move_recv, ghost_send, ghost_recv, name_send, name_recv, bound_send, bound_recv,
     back_send, back_recv, answer,
 ):
@@ -367,12 +367,6 @@
 
     hear(2)
     damping = 4.0 / (3.0 * mine[len(ROUNDS)][0:1, :])
-    for row in range(STORE):
-        value = p_v[row].astype(F32) - damping * inverses[row][0:1, :] * prods[row]
-        outs[row] = jnp.where(row < rows, value, 0.0).astype(BF16)
-    head_copy = load(outs.at[pl.ds(0, STORE)], out_hbm.at[0, 0, pl.ds(0, STORE)], 0)
-    head_copy.start()
-
     for copy in name_copies:
         copy.wait_recv()
     peer_block = [jnp.max(names[i]) for i in range(GRP - 1)]
@@ -389,10 +383,12 @@
         at = position(name)
         return at + jnp.where(at < ONE_WAY, shift[0], jnp.where(at < 2 * ONE_WAY, shift[1], shift[2]))
 
+    back = (back_first, back_second)
+
     def back_copy(n, i):
         rows_of = pl.ds(n * half, half)
         return remote(
-            guest.at[rows_of], back.at[i, rows_of], back_send.at[2 * i + n], back_recv.at[2 * i + n], xs[i]
+            guest.at[rows_of], back[n].at[i], back_send.at[2 * i + n], back_recv.at[2 * i + n], xs[i]
         )
 
     lax.fori_loop(STEPS - LAG, STEPS, lambda t, carry: (await_step(t), carry)[1], 0)
@@ -405,6 +401,12 @@
         for i in (1, 0, 2):
             back_copy(n, i).start()
 
+    for row in range(STORE):
+        value = p_v[row].astype(F32) - damping * inverses[row][0:1, :] * prods[row]
+        outs[row] = jnp.where(row < rows, value, 0.0).astype(BF16)
+    head_copy = load(outs.at[pl.ds(0, STORE)], out_hbm.at[0, 0, pl.ds(0, STORE)], 0)
+    head_copy.start()
+
     def drain(t, carry):
         for way in range(2):
             step_copy(way, t, got.at[way * STEPS + t]).wait_send()
@@ -424,22 +426,26 @@
         for copy in bound_copies(k):
             copy.wait_send()
 
+    tail_copies = []
     for n in range(2):
         for i in range(GRP - 1):
             back_copy(n, i).wait_recv()
-    for b in range((RCAP - STORE) // UNIT):
-        holder = jnp.int32(0)
-        for i in range(GRP - 1):
-            holder = jnp.where(peer_block[i] == b, i, holder)
-        for s in range(UNIT):
-            outs[STORE + b * UNIT + s] = jnp.where(heavy, back[holder, s], jnp.zeros((PC, TB), BF16))
-    tail_copy = load(outs.at[pl.ds(STORE, RCAP - STORE)], out_hbm.at[0, 0, pl.ds(STORE, RCAP - STORE)], 1)
-    tail_copy.start()
+        for b in range((RCAP - STORE) // UNIT):
+            holder = jnp.int32(0)
+            for i in range(GRP - 1):
+                holder = jnp.where(peer_block[i] == b, i, holder)
+            first = STORE + b * UNIT + n * half
+            for s in range(half):
+                outs[first + s] = jnp.where(heavy, back[n][holder, s], jnp.zeros((PC, TB), BF16))
+            copy = load(outs.at[pl.ds(first, half)], out_hbm.at[0, 0, pl.ds(first, half)], 1 + len(tail_copies))
+            copy.start()
+            tail_copies.append(copy)
     for n in range(2):
         for i in range(GRP - 1):
             back_copy(n, i).wait_send()
     head_copy.wait()
-    tail_copy.wait()
+    for copy in tail_copies:
+        copy.wait()
 
 
 def hand_over(source, target, held, sem):
@@ -482,7 +488,8 @@
             pltpu.VMEM((STORE, *tile), F32),
             pltpu.VMEM((STORE, 8, TB), F32),
             pltpu.VMEM((UNIT, *tile), BF16),
-            pltpu.VMEM((GRP - 1, UNIT, *tile), BF16),
+            pltpu.VMEM((GRP - 1, UNIT // 2, *tile), BF16),
+            pltpu.VMEM((GRP - 1, UNIT // 2, *tile), BF16),
             pltpu.VMEM((8, TB), jnp.int32),
             pltpu.VMEM((GRP - 1, 8, TB), jnp.int32),
             pltpu.VMEM((len(ROUNDS) + 1, 8, TB), F32),

time: 41.9 us -> 41.8 us (level)
  no operation moved by 1% of the time
where the time goes in v5:
time: 41.8 us; the launch traced here: 41.4 us
  Pallas kernels  40.1 us (96%)
  between operations  1.3 us (3%)
    pallas_call x1, Pallas kernels, on_device(): pl.pallas_call(kernel, out_shape=jax.ShapeDtypeStruct(p0.shape, p0.dtype)...  38.1 us
    pallas_call x1, Pallas kernels, on_device(): pl.pallas_call(hand_over, out_shape=jax.ShapeDtypeStruct(p0.shape, p0.dty...  1.96 us

profile of v5, /device:TPU:32, one launch (start us, length us, event | category | flops | bytes accessed | tf_op | source)
XLA Modules:
  0.0 41.4 jit_solution(2594856426128170240)
XLA Ops:
  1.3 38.1 %shard_map.82.source = bf16[1,1,36,96,128]{4,3,2,1,0:T(8,128)(2,1)} custom-call(bf16[1,1,18,8,128,128]{5,4,3,2,1,0:T(8,128)(2,1)} %a_hbm.1, s32[1,1,8,18]{3,2,1,0:T(8,128)} %bitcast.2, bf16[1,1,6,8,128,128]{5,4,3,2,1,0:T(8,128)(2,1)} %s_hbm.1, s32[1,6,1,8]{3,2,1,0:T(1,128)} %bitcast.3, s32[1,1]{1,0:T(1,128)S(6)} %copy.9.hosts_hbm, ...), custom_call_target="tpu_custom_call" | custom-call | flops 604000000 | bytes 9000000 | tf_op jit(solution)/shard_map/pallas_call | solution.py:469
  39.4 2.0 %shard_map.83 = bf16[1,1,36,96,128]{4,3,2,1,0:T(8,128)(2,1)} custom-call(bf16[1,1,36,96,128]{4,3,2,1,0:T(8,128)(2,1)} %shard_map.82.source), custom_call_target="tpu_custom_call" | custom-call | tf_op jit(solution)/shard_map/pallas_call | solution.py:524
